TPU v7x, 128 devices: a whole 4x4x4 slice. The times are simulated.
128 devices in a mesh: tile: 32 (over z, x, core), frame: 4 (over y).
Axes of the slice: x: 4, y: 4, z: 4, core: 2. Of those that a mesh axis runs over, the one named last changes fastest.
Arguments:
- cells: bfloat16 [4, 65536, 128], P('frame', 'tile'), may hold values from -24 to 24
- vectors: bfloat16 [8, 128], replicated, may hold values from -6 to 6
- weights: bfloat16 [4, 128, 128], replicated, may hold values from -0.5 to 0.5
- cuboid_shift: int32 [1], replicated, may hold values from 0 to 2047
- cell_upstream: bfloat16 [4, 65536, 128], P('frame', 'tile'), may hold values from -6 to 6
- vector_upstream: float32 [8, 128], replicated, may hold values from -6 to 6
Outputs:
- cell_grad: bfloat16 [4, 65536, 128], P('frame', 'tile')
- weight_grad: float32 [4, 128, 128], replicated
- vector_grad: float32 [8, 128], replicated
All inputs are finite; a program needn't handle non-finite values.
Results may differ from a plain program's by a relative error of at most 0.008.
The roundings to bfloat16 on the way count: a program that leaves them out, or rounds other values in their place, can miss the bound.
Values may be sent and summed in bfloat16 or wider, within the bound.
No kernel may reach another device: no remote copies, remote signals or barrier semaphores. Data moves between devices by JAX's collectives and lax.ppermute only.
A program may use at most 64 MiB of HBM per device.

v0:
```python
import jax
import jax.numpy as jnp
from jax import lax
from jax.sharding import PartitionSpec as P

HEADS = 4
SPAN = 4


highest_precision = lax.Precision.HIGHEST


def to_cuboids(rows):
    tile_count = lax.axis_size("tile")
    frame_count = lax.axis_size("frame")
    columns = rows.shape[-1]
    peer_rows = rows.shape[0] // (tile_count * frame_count)
    moved = lax.all_to_all(
        rows.reshape(tile_count * frame_count, peer_rows, columns),
        ("tile", "frame"),
        split_axis=0,
        concat_axis=0,
        tiled=True,
    )
    moved = moved.reshape(tile_count, frame_count, peer_rows // SPAN, SPAN, columns)
    return moved.transpose(2, 0, 1, 3, 4).reshape(
        peer_rows // SPAN, tile_count * frame_count * SPAN, columns
    )


def from_cuboids(block):
    tile_count = lax.axis_size("tile")
    frame_count = lax.axis_size("frame")
    columns = block.shape[-1]
    cub_count = block.shape[0]
    block = block.reshape(cub_count, tile_count, frame_count, SPAN, columns).transpose(
        1, 2, 0, 3, 4
    )
    moved = lax.all_to_all(
        block.reshape(tile_count * frame_count, cub_count * SPAN, columns),
        ("tile", "frame"),
        split_axis=0,
        concat_axis=0,
        tiled=True,
    )
    return moved.reshape(-1, columns)


def cuboid_pass(query_rows, key_matrix, value_matrix, upstream, global_key, global_value, w_out):
    logit_scale = query_rows.shape[-1] ** (-0.5)
    local_score_rows = (
        jnp.einsum("qnc,inc->nqi", query_rows, key_matrix, preferred_element_type=jnp.float32)
        * logit_scale
    )
    s_global = (
        jnp.einsum("lhd,ghd->hlg", query_rows, global_key, preferred_element_type=jnp.float32)
        * logit_scale
    )
    row_top = jnp.maximum(
        jnp.max(local_score_rows, -1, keepdims=True), jnp.max(s_global, -1, keepdims=True)
    )
    e_local = jnp.exp(local_score_rows - row_top)
    e_global = jnp.exp(s_global - row_top)
    row_total = jnp.sum(e_local, -1, keepdims=True) + jnp.sum(e_global, -1, keepdims=True)
    p_local = e_local / row_total
    p_global = e_global / row_total
    local_probability_rows = p_local.astype(jnp.bfloat16)
    pb_global = p_global.astype(jnp.bfloat16)
    attended_output = jnp.einsum(
        "ofb,bow->fow", local_probability_rows, value_matrix, preferred_element_type=jnp.float32
    )
    attended_output = attended_output + jnp.einsum(
        "hlg,ghd->lhd", pb_global, global_value, preferred_element_type=jnp.float32
    )
    attended_output = attended_output.reshape(attended_output.shape[0], -1).astype(jnp.bfloat16)
    attention_gradient = jnp.einsum(
        "lc,dc->ld", upstream, w_out, preferred_element_type=jnp.float32
    )
    attention_gradient = attention_gradient.astype(jnp.bfloat16).reshape(query_rows.shape)
    local_probability_gradient = jnp.einsum(
        "qnc,inc->nqi", attention_gradient, value_matrix, preferred_element_type=jnp.float32
    )
    dprob_global = jnp.einsum(
        "lhd,ghd->hlg", attention_gradient, global_value, preferred_element_type=jnp.float32
    )
    row_dot = jnp.sum(p_local * local_probability_gradient, -1, keepdims=True) + jnp.sum(
        p_global * dprob_global, -1, keepdims=True
    )
    local_score_gradient = (p_local * (local_probability_gradient - row_dot) * logit_scale).astype(
        jnp.bfloat16
    )
    ds_global = (p_global * (dprob_global - row_dot) * logit_scale).astype(jnp.bfloat16)
    query_gradient = jnp.einsum(
        "ofb,bow->fow", local_score_gradient, key_matrix, preferred_element_type=jnp.float32
    )
    query_gradient = query_gradient + jnp.einsum(
        "hlg,ghd->lhd", ds_global, global_key, preferred_element_type=jnp.float32
    )
    key_gradient = jnp.einsum(
        "yqn,qyk->nyk", local_score_gradient, query_rows, preferred_element_type=jnp.float32
    )
    value_gradient = jnp.einsum(
        "yqn,qyk->nyk",
        local_probability_rows,
        attention_gradient,
        preferred_element_type=jnp.float32,
    )
    grad_gkey = jnp.einsum(
        "hlg,lhd->ghd", ds_global, query_rows, preferred_element_type=jnp.float32
    )
    grad_gvalue = jnp.einsum(
        "hlg,lhd->ghd", pb_global, attention_gradient, preferred_element_type=jnp.float32
    )
    return (
        attended_output,
        query_gradient.astype(jnp.bfloat16),
        key_gradient,
        value_gradient,
        grad_gkey,
        grad_gvalue,
    )


def body(cells, vectors, weights, cuboid_shift, cell_upstream, vector_upstream):
    channels = cells.shape[-1]
    head_dim = channels // HEADS
    vec_count = vectors.shape[0]
    tile_cells = cells.shape[1]
    offset = cuboid_shift[0] * (lax.axis_index("tile") + 1) % tile_cells
    local_cells = jnp.roll(cells[0], -offset, axis=0)
    local_upstream = jnp.roll(cell_upstream[0], -offset, axis=0)
    w_qkv = weights[:3].transpose(1, 0, 2).reshape(channels, 3 * channels)
    w_out = weights[3]
    local_proj = jnp.dot(local_cells, w_qkv, preferred_element_type=jnp.float32).astype(
        jnp.bfloat16
    )
    moved = to_cuboids(jnp.concatenate([local_proj, local_upstream], axis=1))
    projected = moved[..., : 3 * channels]
    cuboid_upstream = moved[..., 3 * channels :]
    cub_count, cub_len = (moved.shape[0], moved.shape[1])
    query_rows = projected[..., :channels].reshape(cub_count, cub_len, HEADS, head_dim)
    key_matrix = projected[..., channels : 2 * channels].reshape(
        cub_count, cub_len, HEADS, head_dim
    )
    value_matrix = projected[..., 2 * channels :].reshape(cub_count, cub_len, HEADS, head_dim)
    global_proj = jnp.dot(vectors, w_qkv, preferred_element_type=jnp.float32).astype(jnp.bfloat16)
    global_proj = global_proj.reshape(vec_count, 3, HEADS, head_dim)
    global_query = global_proj[:, 0]
    global_key = global_proj[:, 1]
    global_value = global_proj[:, 2]
    key_flat = key_matrix.reshape(-1, HEADS, head_dim)
    value_single = value_matrix.reshape(-1, HEADS, head_dim).astype(jnp.float32)
    logit_scale = head_dim ** (-0.5)
    global_score = (
        jnp.einsum("ghd,nhd->hgn", global_query, key_flat, preferred_element_type=jnp.float32)
        * logit_scale
    )
    global_top = lax.pmax(jnp.max(global_score, -1), ("tile", "frame"))
    global_exp = jnp.exp(global_score - global_top[..., None])
    local_numer = jnp.einsum("hgn,nhd->hgd", global_exp, value_single, precision=highest_precision)
    global_total, global_numer = lax.psum((jnp.sum(global_exp, -1), local_numer), ("tile", "frame"))

    def one_cuboid(items):
        return cuboid_pass(items[0], items[1], items[2], items[3], global_key, global_value, w_out)

    attended_output, query_gradient, key_gradient, value_gradient, grad_gkey, grad_gvalue = lax.map(
        one_cuboid, (query_rows, key_matrix, value_matrix, cuboid_upstream)
    )
    global_att = global_numer / global_total[..., None]
    global_prob = global_exp / global_total[..., None]
    grad_global = jnp.dot(vector_upstream, w_out.T.astype(jnp.float32), precision=highest_precision)
    grad_global = grad_global.reshape(vec_count, HEADS, head_dim).transpose(1, 0, 2)
    global_dprob = jnp.einsum(
        "hgd,nhd->hgn", grad_global, value_single, precision=highest_precision
    )
    global_row = jnp.sum(grad_global * global_att, -1)
    global_dscore = global_prob * (global_dprob - global_row[..., None]) * logit_scale
    key_extra = jnp.einsum(
        "hgn,ghd->nhd", global_dscore, global_query.astype(jnp.float32), precision=highest_precision
    )
    value_extra = jnp.einsum("hgn,hgd->nhd", global_prob, grad_global, precision=highest_precision)
    grad_gquery = jnp.einsum(
        "hgn,nhd->hgd", global_dscore, key_flat.astype(jnp.float32), precision=highest_precision
    )
    grad_qkv = jnp.concatenate(
        [
            query_gradient.reshape(cub_count, cub_len, channels),
            (key_gradient + key_extra.reshape(key_gradient.shape))
            .astype(jnp.bfloat16)
            .reshape(cub_count, cub_len, channels),
            (value_gradient + value_extra.reshape(value_gradient.shape))
            .astype(jnp.bfloat16)
            .reshape(cub_count, cub_len, channels),
        ],
        axis=-1,
    )
    flat_grad = from_cuboids(grad_qkv)
    local_grad = jnp.einsum(
        "nk,ck->nc", flat_grad, w_qkv, preferred_element_type=jnp.float32
    ).astype(jnp.bfloat16)
    contract_rows = (((0,), (0,)), ((), ()))
    weight_part = lax.dot_general(
        local_cells, flat_grad, contract_rows, preferred_element_type=jnp.float32
    )
    out_part = lax.dot_general(
        attended_output.reshape(-1, channels),
        cuboid_upstream.reshape(-1, channels),
        contract_rows,
        preferred_element_type=jnp.float32,
    )
    flat_gq = grad_gquery.transpose(1, 0, 2).reshape(vec_count, channels)
    flat_gk = jnp.sum(grad_gkey, 0).reshape(vec_count, channels)
    flat_gv = jnp.sum(grad_gvalue, 0).reshape(vec_count, channels)
    summed_w, summed_g = lax.psum(
        (jnp.concatenate([weight_part, out_part], axis=1), jnp.stack([flat_gq, flat_gk, flat_gv])),
        ("tile", "frame"),
    )
    vector_single = vectors.astype(jnp.float32)
    global_extra = jnp.einsum("gc,sgd->scd", vector_single, summed_g, precision=highest_precision)
    att_flat = global_att.transpose(1, 0, 2).reshape(vec_count, channels)
    out_extra = jnp.dot(att_flat.T, vector_upstream, precision=highest_precision)
    weight_grad = summed_w.reshape(channels, 4, channels).transpose(1, 0, 2) + jnp.concatenate(
        [global_extra, out_extra[None]], 0
    )
    vector_grad = jnp.einsum(
        "sgd,scd->gc", summed_g, weights[:3].astype(jnp.float32), precision=highest_precision
    )
    cell_grad = jnp.roll(local_grad, offset, axis=0)[None]
    return (cell_grad, weight_grad, vector_grad)


def solution(mesh):
    in_specs = (P("frame", "tile", None), P(), P(), P(), P("frame", "tile", None), P())
    out_specs = (P("frame", "tile", None), P(), P())
    return jax.shard_map(body, mesh=mesh, in_specs=in_specs, out_specs=out_specs, check_vma=False)
```

profile of v0, /device:TPU:1, one launch (start us, length us, event | category | flops | bytes accessed | tf_op | source)
XLA Modules:
  0.0 511.4 jit_solution(12427411715972663568)
XLA Ops:
  8.9 1.2 copy.95
  10.6 1.9 convolution_convert_fusion.1
  12.7 2.5 copy.96
  15.2 11.5 %all-to-all-start = ((bf16[128,16,512]{2,1,0:T(8,128)(2,1)}), bf16[128,16,512]{2,1,0:T(8,128)(2,1)S(1)}, u32[]{:S(2)}, u32[]{:S(2)}) async-start(bf16[128,16,512]{2,1,0:T(8,128)(2,1)} %bitcast.252), calls=%async_computation | async-start | bytes 4194304 | tf_op jit(solution)/shard_map/all_to_all | solution.py:18
  29.3 28.0 %all-to-all-done = bf16[128,16,512]{2,1,0:T(8,128)(2,1)S(1)} async-done(((bf16[128,16,512]{2,1,0:T(8,128)(2,1)}), bf16[128,16,512]{2,1,0:T(8,128)(2,1)S(1)}, u32[]{:S(2)}, u32[]{:S(2)}) %all-to-all-start) | async-done | bytes 2097184 | tf_op jit(solution)/shard_map/all_to_all | solution.py:18
  57.3 2.1 reshape.101
  59.3 2.9 copy.97
  63.6 1.1 copy.98
  65.9 62.7 %pmax.7 = f32[4,8]{1,0:T(4,128)S(1)} all-reduce(f32[4,8]{1,0:T(4,128)S(1)} %get-tuple-element.204), channel_id=1, replica_groups=mesh['tile'=32,'frame'=4] {'tile','frame'}, use_global_device_ids=true, to_apply=%region_9.11 | all-reduce | flops 32 | bytes 256 | tf_op jit(solution)/shard_map/pmax | solution.py:158
  129.8 1.2 fusion.58
  131.3 63.3 %all-reduce = (f32[4,8]{1,0:T(4,128)S(1)}, f32[4,8,32]{2,1,0:T(8,128)S(1)}) all-reduce(f32[4,8]{1,0:T(4,128)} %fusion.60, f32[4,8,32]{2,1,0:T(8,128)} %fusion.58), channel_id=1, replica_groups=mesh['tile'=32,'frame'=4] {'tile','frame'}, use_global_device_ids=true, to_apply=%region_11.13 | all-reduce | flops 1056 | bytes 8448 | tf_op jit(solution)/shard_map/psum | solution.py:161
  194.6 2.7 fusion.63
  197.3 1.4 fusion.66
  198.7 1.8 fusion.51
  201.2 49.8 %while.20 = (s32[]{:T(128)}, bf16[4,512,128]{1,2,0:T(8,128)(2,1)}, bf16[4,512,4,32]{1,3,2,0:T(8,128)(2,1)}, f32[4,512,4,32]{1,3,2,0:T(8,128)}, f32[4,512,4,32]{1...) while((s32[]{:T(128)}, bf16[4,512,128]{1,2,0:T(8,128)(2,1)}, ...), condition=%wide.region_7.9_spmd, body=%wide.region_0.8_spmd.sunk | while | flops 452585472 | bytes 46878420 | solution.py:166
  203.1 1.6 fusion.170
  204.7 1.3 multiply_reduce_fusion.9
  206.2 1.3 multiply_convert_fusion.5
  207.5 1.5 fusion.169
  215.5 1.6 fusion.170
  217.2 1.3 multiply_reduce_fusion.9
  218.7 1.3 multiply_convert_fusion.5
  220.0 1.4 fusion.169
  228.0 1.6 fusion.170
  229.6 1.3 multiply_reduce_fusion.9
  231.1 1.3 multiply_convert_fusion.5
  232.4 1.4 fusion.169
  240.4 1.6 fusion.170
  242.0 1.3 multiply_reduce_fusion.9
  243.5 1.3 multiply_convert_fusion.5
  244.8 1.4 fusion.169
  251.6 2.3 fusion.53
  253.9 2.8 copy.110
  256.7 1.8 concatenate.24
  258.4 2.5 fusion.52
  261.0 2.8 copy.112
  263.8 1.7 concatenate.25
  265.5 2.8 copy.105
  268.3 1.8 concatenate.23
  270.1 2.3 maximum_bitcast_fusion
  273.2 1.4 reshape.109
  274.6 5.0 all-to-all-start.1
  282.3 73.4 %psum.31 = f32[3,8,128]{2,1,0:T(8,128)S(1)} all-reduce(f32[3,8,128]{2,1,0:T(8,128)S(1)} %pad_maximum_fusion.2), channel_id=1, replica_groups=mesh['tile'=32,'frame'=4] {'tile','frame'}, use_global_device_ids=true, to_apply=%region_17.19 | all-reduce | flops 3072 | bytes 24576 | tf_op jit(solution)/shard_map/psum | solution.py:214
  356.1 1.7 convolution_bitcast_fusion.13
  357.8 1.3 convolution_bitcast_fusion.10
  359.5 2.2 fusion.70
  363.2 2.8 fusion.55
  365.9 136.8 %all-reduce.3.cloned.1.call-done = f32[4,128,128]{1,2,0:T(8,128)} async-done(((f32[4,128,128]{1,2,0:T(8,128)}), f32[4,128,128]{1,2,0:T(8,128)}) %all-reduce.3.cloned.1.call-update) | async-done | bytes 262160 | tf_op jit(solution)/shard_map/psum | solution.py:214
  (150 shorter events, 43.4 us)
Async XLA Ops:
  7.2 21.3 %copy-start = (f32[8,128]{1,0:T(8,128)S(1)}, f32[8,128]{1,0:T(8,128)}, u32[]{:S(2)}) copy-start(f32[8,128]{1,0:T(8,128)} %param.15) | copy-start | bytes 12292
  12.7 14.1 %copy-start.8 = (bf16[8,128]{1,0:T(8,128)(2,1)S(1)}, bf16[8,128]{1,0:T(8,128)(2,1)}, u32[]{:S(2)}) copy-start(bf16[8,128]{1,0:T(8,128)(2,1)} %param.11) | copy-start | bytes 6148
  15.2 42.1 %all-to-all-start = ((bf16[128,16,512]{2,1,0:T(8,128)(2,1)}), bf16[128,16,512]{2,1,0:T(8,128)(2,1)S(1)}, u32[]{:S(2)}, u32[]{:S(2)}) async-start(bf16[128,16,512]{2,1,0:T(8,128)(2,1)} %bitcast.252), calls=%async_computation | async-start | bytes 4194304 | tf_op jit(solution)/shard_map/all_to_all | solution.py:18
  27.0 38.6 %copy-start.5 = (bf16[8,1,4,32]{3,2,1,0:T(4,128)(2,1)}, bf16[8,1,4,32]{3,2,1,0:T(4,128)(2,1)S(1)}, u32[]{:S(2)}) copy-start(bf16[8,1,4,32]{3,2,1,0:T(4,128)(2,1)S(1)} %get-tuple-element.199) | copy-start | bytes 6148
  201.1 49.9 %copy-start.1 = (f32[4,8,2048]{2,1,0:T(8,128)S(1)}, f32[4,8,2048]{2,1,0:T(8,128)}, u32[]{:S(2)}) copy-start(f32[4,8,2048]{2,1,0:T(8,128)} %fusion.51) | copy-start | bytes 786436
  201.1 49.8 %copy-start.6 = (bf16[8,1,4,32]{3,2,1,0:T(4,128)(2,1)S(1)}, bf16[8,1,4,32]{3,2,1,0:T(4,128)(2,1)}, u32[]{:S(2)}) copy-start(bf16[8,1,4,32]{3,2,1,0:T(4,128)(2,1)} %copy-done.5) | copy-start | bytes 6148
  203.1 1.7 copy-start.3
  204.7 1.3 copy-start.4
  215.5 1.6 copy-start.3
  217.2 1.3 copy-start.4
  228.0 1.6 copy-start.3
  229.6 1.3 copy-start.4
  240.4 1.6 copy-start.3
  242.0 1.3 copy-start.4
  273.2 9.0 %copy-start.7 = (f32[8,4,32]{2,0,1:T(8,128)S(1)}, f32[8,4,32]{2,0,1:T(8,128)}, u32[]{:S(2)}) copy-start(f32[8,4,32]{2,0,1:T(8,128)} %get-tuple-element.202) | copy-start | bytes 12292
  273.2 85.9 %copy-start.9 = (bf16[8,128]{1,0:T(8,128)(2,1)S(1)}, bf16[8,128]{1,0:T(8,128)(2,1)}, u32[]{:S(2)}) copy-start(bf16[8,128]{1,0:T(8,128)(2,1)} %param.11) | copy-start | bytes 6148
  273.2 86.3 %copy-start.2 = (bf16[1,2048,128]{2,1,0:T(8,128)(2,1)S(1)}, bf16[1,2048,128]{2,1,0:T(8,128)(2,1)}, u32[]{:S(2)}) copy-start(bf16[1,2048,128]{2,1,0:T(8,128)(2,1)} %param.10) | copy-start | bytes 1572868
  274.6 84.9 %all-to-all-start.1 = ((bf16[128,16,384]{2,1,0:T(8,128)(2,1)}), bf16[128,16,384]{2,1,0:T(8,128)(2,1)S(1)}, u32[]{:S(2)}, u32[]{:S(2)}) async-start(bf16[128,16,384]{2,1,0:T(8,128)(2,1)} %reshape.109), calls=%async_computation.1 | async-start | bytes 3145728 | tf_op jit(solution)/shard_map/all_to_all | solution.py:39
  279.6 223.1 %all-reduce.3.cloned.1.call-start = ((), (), s32[]{:S(2)}) async-start(), calls=%async_computation.2 | async-start | bytes 524288 | tf_op jit(solution)/shard_map/psum | solution.py:214
Sparse Core Ops, SparseCore 0:
  363.3 139.3 all-reduce.2
where the time goes:
time: 513 us; the launch traced here: 511 us
  blocking collectives  199 us (39%)
  waiting for transfers between devices  165 us (32%)
  matrix products  54.8 us (11%)
  local copies, waits for them, and re-layouts  36.6 us (7%)
  other arithmetic  23.6 us (5%)
  starting transfers between devices  16.6 us (3%)
  between operations  15.2 us (3%)
    psum x1, waiting for transfers between devices, body(): lax.psum((jnp.concatenate([weight_part, out_part], axis=1), jnp.stack([fl...  137 us
    psum x1, blocking collectives, body(): lax.psum((jnp.concatenate([weight_part, out_part], axis=1), jnp.stack([fl...  73.4 us
    psum x1, blocking collectives, body(): lax.psum((jnp.sum(global_exp, -1), local_numer), ('tile', 'frame'))  63.3 us
    pmax x1, blocking collectives, body(): global_top = lax.pmax(jnp.max(global_score, -1), ('tile', 'frame'))  62.7 us
    all_to_all x1, waiting for transfers between devices, to_cuboids(): lax.all_to_all(rows.reshape(tile_count * frame_count, peer_rows, columns)...  28 us
    all_to_all x1, starting transfers between devices, to_cuboids(): lax.all_to_all(rows.reshape(tile_count * frame_count, peer_rows, columns)...  11.5 us
  transfers between devices with their start and end apart: 3, of which 2 were waited for; matrix products, arithmetic and copies ran while one was open for 2% of the time, Pallas kernels for 0%

commit v1 on v0

v1 whole, which is shorter than its diff:
```python
import math

import jax
import jax.numpy as jnp
from jax import lax
from jax.experimental import pallas as pl
from jax.experimental.pallas import tpu as pltpu
from jax.sharding import PartitionSpec as P

CH = 128
HEADS = 4
HDIM = 32
GLOBALS = 8
PAIRS = HEADS * GLOBALS
SPAN = 4
CELLS_DEV = 2048
PEERS = 128
PEER_ROWS = CELLS_DEV // PEERS
CUBOIDS = PEER_ROWS // SPAN
TOKENS = 512
GROUP = 16
GROUP_ROWS = GROUP * PEER_ROWS
WINDOW = GROUP_ROWS + 16
MSG_ROWS = 40
SCALE = HDIM**-0.5
LOG2E = math.log2(math.e)
BF = jnp.bfloat16
F32 = jnp.float32
HIGHEST = lax.Precision.HIGHEST
NT = (((1,), (1,)), ((), ()))


def dot(a, b):
    return jnp.dot(a, b, preferred_element_type=F32)


def dot_nt(a, b):
    return lax.dot_general(a, b, NT, preferred_element_type=F32)


def iota(shape, axis):
    return lax.broadcasted_iota(jnp.int32, shape, axis)


def split3(x):
    hi = x.astype(BF)
    rest = x - hi.astype(F32)
    mid = rest.astype(BF)
    low = (rest - mid.astype(F32)).astype(BF)
    return hi, mid, low


def head_blocks(rows):
    head = iota((GLOBALS, CH), 1) // HDIM
    return jnp.concatenate([jnp.where(head == h, rows, 0.0) for h in range(HEADS)], axis=0)


def head_diagonal(blocks):
    head = iota((GLOBALS, CH), 1) // HDIM
    total = jnp.zeros((GLOBALS, CH), F32)
    for h in range(HEADS):
        total += jnp.where(head == h, blocks[h * GLOBALS : (h + 1) * GLOBALS], 0.0)
    return total


def global_rows(vectors, weight):
    return dot(vectors.astype(BF), weight).astype(BF).astype(F32)


def global_upstream(vector_upstream, w_out):
    hi, mid, low = split3(vector_upstream)
    return dot_nt(hi, w_out) + dot_nt(mid, w_out) + dot_nt(low, w_out)


def tile_offset(shift_ref):
    return (shift_ref[0] * (lax.axis_index("tile") + 1)) % CELLS_DEV


def shift_matrix(step):
    return (iota((GROUP_ROWS, WINDOW), 1) == iota((GROUP_ROWS, WINDOW), 0) + step).astype(BF)


def pack_kernel(
    shift_ref, cells_ref, up_ref, vectors_ref, weights_ref, vup_ref, msg_ref, held
):
    held[:CELLS_DEV, :CH] = cells_ref[...]
    held[:CELLS_DEV, CH:] = up_ref[...]
    held[CELLS_DEV:, :CH] = cells_ref[:WINDOW]
    held[CELLS_DEV:, CH:] = up_ref[:WINDOW]
    offset = tile_offset(shift_ref)
    mover = shift_matrix(offset % 16)
    base = offset - offset % 16
    for i in range(CELLS_DEV // GROUP_ROWS):
        start = pl.multiple_of((base + i * GROUP_ROWS) % CELLS_DEV, 16)
        moved = dot(mover, held[pl.ds(start, WINDOW), :]).astype(BF)
        peers = pl.ds(i * GROUP, GROUP)
        msg_ref[peers, 0:PEER_ROWS, :] = moved[:, :CH].reshape(GROUP, PEER_ROWS, CH)
        msg_ref[peers, PEER_ROWS : 2 * PEER_ROWS, :] = moved[:, CH:].reshape(GROUP, PEER_ROWS, CH)
    vectors = vectors_ref[...]
    query = head_blocks(global_rows(vectors, weights_ref[0])).astype(BF)
    upstream = head_blocks(global_upstream(vup_ref[...], weights_ref[3]))
    up_parts = jnp.concatenate([part.astype(F32) for part in split3(upstream)], axis=0).astype(BF)
    keys = dot(cells_ref[...], weights_ref[1]).astype(BF)
    values = dot(cells_ref[...], weights_ref[2]).astype(BF)
    score = dot_nt(query, keys) * SCALE
    dprob = dot_nt(up_parts, values)
    dprob = dprob[:PAIRS] + dprob[PAIRS : 2 * PAIRS] + dprob[2 * PAIRS :]
    top = jnp.max(score, axis=1, keepdims=True)
    weight = jnp.exp(score - top)
    total = jnp.sum(weight, axis=1, keepdims=True)
    inner = jnp.sum(weight * dprob, axis=1, keepdims=True)
    lane = iota((PAIRS, CH), 1)
    stats = jnp.where(lane == 0, top, jnp.where(lane == 1, total, jnp.where(lane == 2, inner, 0.0)))
    parts = [part.astype(F32) for part in split3(stats)] + [jnp.zeros((PAIRS, CH), F32)]
    rows = jnp.concatenate(parts, axis=0).T[:GLOBALS].astype(BF)
    msg_ref[:, 2 * PEER_ROWS :, :] = jnp.broadcast_to(rows[None], (PEERS, GLOBALS, CH))


def regroup_matrix():
    row = iota((GROUP_ROWS, GROUP_ROWS), 0)
    column = iota((GROUP_ROWS, GROUP_ROWS), 1)
    source = (row // SPAN) % GROUP * PEER_ROWS + row // (GROUP * SPAN) * SPAN + row % SPAN
    return (column == source).astype(BF)


def back_matrix():
    row = iota((GROUP_ROWS, GROUP_ROWS), 0)
    column = iota((GROUP_ROWS, GROUP_ROWS), 1)
    source = (row // SPAN) % CUBOIDS * (GROUP * SPAN) + row // PEER_ROWS * SPAN + row % SPAN
    return (column == source).astype(BF)


def owner_kernel(
    recv_ref,
    vectors_ref,
    weights_ref,
    vup_ref,
    msg_ref,
    cells_ref,
    up_ref,
    delta_ref,
    weights_t_ref,
    query_m,
    grad_m,
    w_sum,
    g_sum,
    part_ref,
):
    group_tokens = GROUP * SPAN
    mover = regroup_matrix()
    for i in range(PEERS // GROUP):
        peers = pl.ds(i * GROUP, GROUP)
        rows = jnp.concatenate(
            [
                recv_ref[peers, 0:PEER_ROWS, :].reshape(GROUP_ROWS, CH),
                recv_ref[peers, PEER_ROWS : 2 * PEER_ROWS, :].reshape(GROUP_ROWS, CH),
            ],
            axis=1,
        )
        moved = dot(mover, rows).astype(BF)
        for u in range(CUBOIDS):
            piece = moved[u * group_tokens : (u + 1) * group_tokens]
            cells_ref[u, pl.ds(i * group_tokens, group_tokens), :] = piece[:, :CH]
            up_ref[u, pl.ds(i * group_tokens, group_tokens), :] = piece[:, CH:]

    stats = recv_ref[:, 2 * PEER_ROWS :, :].astype(F32).reshape(PEERS * GLOBALS, CH)
    stats = stats + pltpu.roll(stats, CH - PAIRS, 1) + pltpu.roll(stats, CH - 2 * PAIRS, 1)
    stats = stats.reshape(PEERS, GLOBALS, CH)
    tops = stats[:, 0:1, :]
    top = jnp.max(tops, axis=0)
    summed = jnp.sum(jnp.exp(tops - top[None]) * stats, axis=0)
    row = iota((GLOBALS, CH), 0)
    lanes = jnp.where(row == 0, top, summed)
    columns = jnp.concatenate([lanes, jnp.zeros((CH - GLOBALS, CH), F32)], axis=0).T
    g_top = columns[:PAIRS, 0:1]
    g_inv = 1.0 / columns[:PAIRS, 1:2]
    g_row = columns[:PAIRS, 2:3] * g_inv

    vectors = vectors_ref[...]
    w_q, w_k, w_v, w_o = (weights_ref[i] for i in range(4))
    for i in range(3):
        weights_t_ref[i] = weights_ref[i].astype(F32).T.astype(BF)
    gq = head_blocks(global_rows(vectors, w_q))
    gk = head_blocks(global_rows(vectors, w_k))
    gv = head_blocks(global_rows(vectors, w_v))
    gg = head_blocks(global_upstream(vup_ref[...], w_o))

    def wide_t(blocks):
        return jnp.concatenate([blocks, jnp.zeros((CH - PAIRS, CH), F32)], axis=0).T

    gq_b, gk_b, gv_b = (x.astype(BF) for x in (gq, gk, gv))
    gk_t = wide_t(gk)[:, :PAIRS].astype(BF)
    gv_t = wide_t(gv)[:, :PAIRS].astype(BF)
    gg3 = [part.astype(F32) for part in split3(gg)]
    gg_parts = jnp.concatenate(gg3, axis=0).astype(BF)
    zero = jnp.zeros((PAIRS, CH), F32)
    gq_t3 = jnp.concatenate([gq, gq, gq, zero], axis=0).T.astype(BF)
    gg_t6a = jnp.concatenate([gg3[0], gg3[0], gg3[0], gg3[1]], axis=0).T.astype(BF)
    gg_t6b = jnp.concatenate([gg3[1], gg3[2], zero, zero], axis=0).T.astype(BF)

    query_m[...] = jnp.zeros_like(query_m)
    grad_m[...] = jnp.zeros_like(grad_m)
    w_sum[...] = jnp.zeros_like(w_sum)
    g_sum[...] = jnp.zeros_like(g_sum)

    def one_cuboid(u, carry):
        cells = cells_ref[u]
        upstream = up_ref[u]
        query_t = dot_nt(weights_t_ref[0], cells).astype(BF)
        key_t = dot_nt(weights_t_ref[1], cells).astype(BF)
        value_t = dot_nt(weights_t_ref[2], cells).astype(BF)
        grad_t = dot_nt(w_o, upstream).astype(BF)
        query = dot(cells, w_q).astype(BF)
        key = dot(cells, w_k).astype(BF)
        value = dot(cells, w_v).astype(BF)
        grad = dot_nt(upstream, w_o).astype(BF)
        for h in range(HEADS):
            part = slice(h * HDIM, (h + 1) * HDIM)
            query_m[h, part, :] = query_t[part]
            grad_m[h, part, :] = grad_t[part]
        s_global = dot(gk_b, query_t)
        d_global = dot(gv_b, grad_t)
        p_rows, ds_rows, out_t, dq_t, dk_t, dv_t = [], [], [], [], [], []
        for h in range(HEADS):
            part = slice(h * HDIM, (h + 1) * HDIM)
            pair = slice(h * GLOBALS, (h + 1) * GLOBALS)
            score = dot(key, query_m[h])
            dprob = dot(value, grad_m[h])
            top = jnp.maximum(
                jnp.max(score, axis=0, keepdims=True),
                jnp.max(s_global[pair], axis=0, keepdims=True),
            )
            e_local = jnp.exp2((score - top) * (SCALE * LOG2E))
            e_global = jnp.exp2((s_global[pair] - top) * (SCALE * LOG2E))
            total = jnp.sum(e_local, axis=0, keepdims=True) + jnp.sum(
                e_global, axis=0, keepdims=True
            )
            inv = 1.0 / total
            p_local = e_local * inv
            p_global = e_global * inv
            inner = jnp.sum(p_local * dprob, axis=0, keepdims=True) + jnp.sum(
                p_global * d_global[pair], axis=0, keepdims=True
            )
            p_low = p_local.astype(BF)
            ds_low = (p_local * (dprob - inner) * SCALE).astype(BF)
            p_rows.append(p_global)
            ds_rows.append(p_global * (d_global[pair] - inner) * SCALE)
            out_t.append(dot(value_t[part], p_low))
            dq_t.append(dot(key_t[part], ds_low))
            dv_t.append(dot_nt(grad_t[part], p_low))
            dk_t.append(dot_nt(query_t[part], ds_low))
        p_rows = jnp.concatenate(p_rows, axis=0).astype(BF)
        ds_rows = jnp.concatenate(ds_rows, axis=0).astype(BF)
        out_t = (jnp.concatenate(out_t, axis=0) + dot(gv_t, p_rows)).astype(BF)
        dq_t = (jnp.concatenate(dq_t, axis=0) + dot(gk_t, ds_rows)).astype(BF)

        prob = jnp.exp(dot(gq_b, key_t) * SCALE - g_top) * g_inv
        g_dprob = dot(gg_parts, value_t)
        g_dprob = g_dprob[:PAIRS] + g_dprob[PAIRS : 2 * PAIRS] + g_dprob[2 * PAIRS :]
        dscore = prob * (g_dprob - g_row) * SCALE
        none = jnp.zeros((PAIRS, TOKENS), BF)
        p_hi, p_mid, p_low3 = split3(prob)
        d_hi, d_mid, d_low3 = split3(dscore)
        d_parts = jnp.concatenate([d_hi, d_mid, d_low3, none], axis=0)
        p_parts = jnp.concatenate([p_hi, p_mid, p_low3, p_hi], axis=0)
        p_more = jnp.concatenate([p_mid, p_hi, none, none], axis=0)
        dk_t = (jnp.concatenate(dk_t, axis=0) + dot(gq_t3, d_parts)).astype(BF)
        dv_t = (
            jnp.concatenate(dv_t, axis=0) + (dot(gg_t6a, p_parts) + dot(gg_t6b, p_more))
        ).astype(BF)
        g_query = dot(d_parts[: 3 * PAIRS], key)
        g_att = dot(p_parts[: 3 * PAIRS], value)
        g_sum[0] += g_query[:PAIRS] + g_query[PAIRS : 2 * PAIRS] + g_query[2 * PAIRS :]
        g_sum[1] += dot(ds_rows, query)
        g_sum[2] += dot(p_rows, grad)
        g_sum[3] += g_att[:PAIRS] + g_att[PAIRS : 2 * PAIRS] + g_att[2 * PAIRS :]
        w_sum[0] += dot(dq_t, cells)
        w_sum[1] += dot(dk_t, cells)
        w_sum[2] += dot(dv_t, cells)
        w_sum[3] += dot(out_t, upstream)
        delta = dot(w_q, dq_t) + dot(w_k, dk_t) + dot(w_v, dv_t)
        delta_ref[u] = delta.T.astype(BF)
        return carry

    lax.fori_loop(0, CUBOIDS, one_cuboid, 0)

    def outer(a, b):
        a = jnp.concatenate([a, jnp.zeros((CH - GLOBALS, CH), F32)], axis=0).T
        b = jnp.concatenate([b, jnp.zeros((CH - GLOBALS, CH), F32)], axis=0)
        return jnp.dot(a, b, precision=HIGHEST, preferred_element_type=F32)

    vec = jnp.zeros((GLOBALS, CH), F32)
    for i in range(4):
        g_part = head_diagonal(g_sum[i])
        if i < 3:
            total = w_sum[i].T + outer(vectors, g_part)
            hi, mid, low = split3(g_part)
            weight = weights_ref[i]
            vec += dot_nt(hi, weight) + dot_nt(mid, weight) + dot_nt(low, weight)
        else:
            total = w_sum[3] + outer(g_part, vup_ref[...])
        hi, mid, low = split3(total)
        rows = pl.ds(i * CH, CH)
        part_ref[0, rows, :] = hi
        part_ref[1, rows, :] = mid
        part_ref[2, rows, :] = low
    vec_parts = jnp.concatenate(
        [x.astype(F32) for x in split3(vec)] + [jnp.zeros((CH - 3 * GLOBALS, CH), F32)], axis=0
    ).T.astype(BF)
    spread = (iota((TOKENS, CH), 0) // SPAN == iota((TOKENS, CH), 1)).astype(BF)
    part_ref[3] = dot(spread, vec_parts).astype(BF)

    back = back_matrix()
    for i in range(PEERS // GROUP):
        peers = pl.ds(i * GROUP, GROUP)
        tokens = pl.ds(i * group_tokens, group_tokens)
        rows = jnp.concatenate(
            [
                jnp.concatenate([delta_ref[u, tokens, :] for u in range(CUBOIDS)], axis=0),
                jnp.concatenate([part_ref[u, tokens, :] for u in range(CUBOIDS)], axis=0),
            ],
            axis=1,
        )
        moved = dot(back, rows).astype(BF)
        msg_ref[peers, 0:PEER_ROWS, :] = moved[:, :CH].reshape(GROUP, PEER_ROWS, CH)
        msg_ref[peers, PEER_ROWS:, :] = moved[:, CH:].reshape(GROUP, PEER_ROWS, CH)


def sum_kernel(recv_ref, piece_ref):
    summed = jnp.sum(recv_ref[:, PEER_ROWS:, :].astype(F32), axis=0)
    weight = summed[0:SPAN] + summed[SPAN : 2 * SPAN] + summed[2 * SPAN : 3 * SPAN]
    last = summed[3 * SPAN :]
    last = last + pltpu.roll(last, CH - GLOBALS, 1) + pltpu.roll(last, CH - 2 * GLOBALS, 1)
    piece = jnp.concatenate([weight, last], axis=0)
    piece_ref[...] = jnp.broadcast_to(piece[None], piece_ref.shape)


def place_kernel(shift_ref, recv_ref, out_ref, held):
    for i in range(PEERS // GROUP):
        held[pl.ds(i * GROUP_ROWS, GROUP_ROWS), :] = recv_ref[
            pl.ds(i * GROUP, GROUP), 0:PEER_ROWS, :
        ].reshape(GROUP_ROWS, CH)
    held[CELLS_DEV:, :] = held[:WINDOW, :]
    offset = (CELLS_DEV - tile_offset(shift_ref)) % CELLS_DEV
    mover = shift_matrix(offset % 16)
    base = offset - offset % 16
    for i in range(CELLS_DEV // GROUP_ROWS):
        start = pl.multiple_of((base + i * GROUP_ROWS) % CELLS_DEV, 16)
        moved = dot(mover, held[pl.ds(start, WINDOW), :]).astype(BF)
        out_ref[pl.ds(i * GROUP_ROWS, GROUP_ROWS), :] = moved


VMEM = pl.BlockSpec(memory_space=pltpu.VMEM)
SMEM = pl.BlockSpec(memory_space=pltpu.SMEM)
PARAMS = pltpu.CompilerParams(vmem_limit_bytes=48 * 1024 * 1024)


def exchange(rows):
    return lax.all_to_all(rows, ("tile", "frame"), split_axis=0, concat_axis=0, tiled=True)


def body(cells, vectors, weights, cuboid_shift, cell_upstream, vector_upstream):
    vectors = vectors.astype(F32)
    message = pl.pallas_call(
        pack_kernel,
        out_shape=jax.ShapeDtypeStruct((PEERS, MSG_ROWS, CH), BF),
        in_specs=[SMEM] + [VMEM] * 5,
        out_specs=VMEM,
        scratch_shapes=[pltpu.VMEM((CELLS_DEV + WINDOW, 2 * CH), BF)],
        compiler_params=PARAMS,
        name="pack",
    )(cuboid_shift, cells[0], cell_upstream[0], vectors, weights, vector_upstream)
    received = exchange(message)
    message = pl.pallas_call(
        owner_kernel,
        out_shape=jax.ShapeDtypeStruct((PEERS, 2 * PEER_ROWS, CH), BF),
        in_specs=[VMEM] * 4,
        out_specs=VMEM,
        scratch_shapes=[
            pltpu.VMEM((CUBOIDS, TOKENS, CH), BF),
            pltpu.VMEM((CUBOIDS, TOKENS, CH), BF),
            pltpu.VMEM((CUBOIDS, TOKENS, CH), BF),
            pltpu.VMEM((3, CH, CH), BF),
            pltpu.VMEM((HEADS, CH, TOKENS), BF),
            pltpu.VMEM((HEADS, CH, TOKENS), BF),
            pltpu.VMEM((4, CH, CH), F32),
            pltpu.VMEM((4, PAIRS, CH), F32),
            pltpu.VMEM((4, TOKENS, CH), BF),
        ],
        compiler_params=PARAMS,
        name="owner",
    )(received, vectors, weights, vector_upstream)
    received = exchange(message)
    pieces = pl.pallas_call(
        sum_kernel,
        out_shape=jax.ShapeDtypeStruct((PEERS, GLOBALS, CH), F32),
        in_specs=[VMEM],
        out_specs=VMEM,
        compiler_params=PARAMS,
        name="sum_pieces",
    )(received)
    pieces = exchange(pieces)
    cell_grad = pl.pallas_call(
        place_kernel,
        out_shape=jax.ShapeDtypeStruct((CELLS_DEV, CH), BF),
        in_specs=[SMEM, VMEM],
        out_specs=VMEM,
        scratch_shapes=[pltpu.VMEM((CELLS_DEV + WINDOW, CH), BF)],
        compiler_params=PARAMS,
        name="place",
    )(cuboid_shift, received)
    weight_grad = pieces[:, :SPAN, :].reshape(4, CH, CH)
    vector_grad = pieces[:, SPAN, :GLOBALS].T
    return cell_grad[None], weight_grad, vector_grad


def solution(mesh):
    in_specs = (P("frame", "tile", None), P(), P(), P(), P("frame", "tile", None), P())
    out_specs = (P("frame", "tile", None), P(), P())
    return jax.shard_map(body, mesh=mesh, in_specs=in_specs, out_specs=out_specs, check_vma=False)
```

time: 513 us -> 110 us (0.21)
  waiting for transfers between devices: 165 us -> 12.5 us
  blocking collectives: 199 us -> 56.6 us
  matrix products: 54.8 us -> 0 us
  local copies, waits for them, and re-layouts: 36.6 us -> 5.14 us
  Pallas kernels: 0 us -> 29.8 us
  other arithmetic: 23.6 us -> 0.68 us
  between operations: 15.2 us -> 1.33 us
  starting transfers between devices: 16.6 us -> 3.81 us
    psum x1 -> x0, waiting for transfers between devices: 137 us -> none  [body(): lax.psum((jnp.concatenate([weight_part, out_part], axis=1), jnp.stack([fl...]
    psum x2 -> x0, blocking collectives: 137 us -> none  [the longest x1 73.4 us: body(): lax.psum((jnp.concatenate([weight_part, out_part], axis=1), jnp.stack([fl...]
    pmax x1 -> x0, blocking collectives: 62.7 us -> none  [body(): global_top = lax.pmax(jnp.max(global_score, -1), ('tile', 'frame'))]
    all_to_all x0 -> x2, blocking collectives: none -> 56.6 us  [exchange(): lax.all_to_all(rows, ('tile', 'frame'), split_axis=0, concat_axis=0, tile...]
    dot_general x67 -> x0, matrix products: 54.8 us -> none  [the longest x4 6.53 us: cuboid_pass(): jnp.einsum('yqn,qyk->nyk', local_probability_rows, attention_gradient, pr...]
    pallas_call x0 -> x4, Pallas kernels: none -> 29.8 us  [the longest x1 25.6 us: body(): pl.pallas_call(owner_kernel, out_shape=jax.ShapeDtypeStruct((PEERS, 2 * P...]
    all_to_all x2 -> x1, waiting for transfers between devices: 28 us -> 12.5 us  [exchange(): lax.all_to_all(rows, ('tile', 'frame'), split_axis=0, concat_axis=0, tile...]
    all_to_all x2 -> x1, starting transfers between devices: 16.5 us -> 3.81 us  [exchange(): lax.all_to_all(rows, ('tile', 'frame'), split_axis=0, concat_axis=0, tile...]
  transfers between devices with their start and end apart: 3 -> 1, of which waited for: 2 -> 1; matrix products, arithmetic and copies ran while one was open for 2% -> 0% of each run, Pallas kernels for 0% -> 1%
where the time goes in v1:
time: 110 us
  blocking collectives  56.6 us (51%)
  Pallas kernels  29.8 us (27%)
  waiting for transfers between devices  12.5 us (11%)
  local copies, waits for them, and re-layouts  5.14 us (5%)
  starting transfers between devices  3.81 us (3%)
  between operations  1.33 us (1%)
    all_to_all x2, blocking collectives, exchange(): lax.all_to_all(rows, ('tile', 'frame'), split_axis=0, concat_axis=0, tile...  56.6 us
    pallas_call x1, Pallas kernels, body(): pl.pallas_call(owner_kernel, out_shape=jax.ShapeDtypeStruct((PEERS, 2 * P...  25.6 us
    all_to_all x1, waiting for transfers between devices, exchange(): lax.all_to_all(rows, ('tile', 'frame'), split_axis=0, concat_axis=0, tile...  12.5 us
    unnamed x13, local copies, waits for them, and re-layouts  4.35 us
    all_to_all x1, starting transfers between devices, exchange(): lax.all_to_all(rows, ('tile', 'frame'), split_axis=0, concat_axis=0, tile...  3.81 us
  transfers between devices with their start and end apart: 1, of which 1 were waited for; matrix products, arithmetic and copies ran while one was open for 0% of the time, Pallas kernels for 1%

profile of v1, /device:TPU:1, one launch (start us, length us, event | category | flops | bytes accessed | tf_op | source)
XLA Modules:
  0.0 109.8 jit_solution(17468226854362593771)
XLA Ops:
  1.3 0.7 convert_element_type.3.vectors_ref
  2.0 0.0 copy-start
  2.0 0.9 copy-done
  2.9 0.0 copy-start.2
  2.9 1.0 copy-done.2
  3.9 0.0 copy-start.3
  3.9 1.0 copy-done.3
  5.0 0.0 copy-start.4
  5.0 0.7 copy-done.4
  5.6 1.7 %pack.1 = bf16[128,40,128]{2,1,0:T(8,128)(2,1)S(1)} custom-call(s32[1]{0:T(128)S(6)} %copy.10.shift_ref, bf16[2048,128]{1,0:T(8,128)(2,1)S(1)} %bitcast.7, bf16[2048,128]{1,0:T(8,128)(2,1)S(1)} %bitcast.8, f32[8,128]{1,0:T(8,128)S(1)} %convert_element_type.3.vectors_ref, bf16[4,128,128]{2,1,0:T(8,128)(2,1)S(1)} %copy-done, f32[8,128]{1,0:T(8,128)S(1)} %copy-done.4), custom_call_target="tpu_custom_call" | custom-call | tf_op jit(solution)/shard_map/pack/pallas_call | solution.py:364
  7.4 0.0 copy-start.1
  7.4 0.0 copy-start.5
  7.4 33.5 %all_to_all.15.recv_ref = bf16[128,40,128]{2,1,0:T(8,128)(2,1)S(1)} all-to-all(bf16[128,40,128]{2,1,0:T(8,128)(2,1)S(1)} %pack.1), channel_id=1, replica_groups=mesh['tile'=32,'frame'=4] {'tile','frame'}, dimensions={0} | all-to-all | bytes 2621440 | tf_op jit(solution)/shard_map/all_to_all | solution.py:359
  40.9 0.0 copy-done.1
  40.9 0.0 copy-done.5
  40.9 25.6 %owner.1 = bf16[128,32,128]{2,1,0:T(8,128)(2,1)S(1)} custom-call(bf16[128,40,128]{2,1,0:T(8,128)(2,1)S(1)} %all_to_all.15.recv_ref, f32[8,128]{1,0:T(8,128)S(1)} %convert_element_type.3.vectors_ref, bf16[4,128,128]{2,1,0:T(8,128)(2,1)S(1)} %copy-done.1, f32[8,128]{1,0:T(8,128)S(1)} %copy-done.5), custom_call_target="tpu_custom_call" | custom-call | tf_op jit(solution)/shard_map/owner/pallas_call | solution.py:374
  66.5 23.1 %all_to_all.16.recv_ref = bf16[128,32,128]{2,1,0:T(8,128)(2,1)S(1)} all-to-all(bf16[128,32,128]{2,1,0:T(8,128)(2,1)S(1)} %owner.1), channel_id=1, replica_groups=mesh['tile'=32,'frame'=4] {'tile','frame'}, dimensions={0} | all-to-all | bytes 2097152 | tf_op jit(solution)/shard_map/all_to_all | solution.py:359
  89.6 1.0 sum_pieces.1
  90.6 3.8 %all-to-all-start.2 = ((f32[128,8,128]{2,1,0:T(8,128)}), f32[128,8,128]{2,1,0:T(8,128)S(1)}, u32[]{:S(2)}, u32[]{:S(2)}) async-start(f32[128,8,128]{2,1,0:T(8,128)} %sum_pieces.1), calls=%async_computation.2 | async-start | bytes 1048576 | tf_op jit(solution)/shard_map/all_to_all | solution.py:359
  94.4 1.4 %place.1 = bf16[2048,128]{1,0:T(8,128)(2,1)} custom-call(s32[1]{0:T(128)S(6)} %copy.10.shift_ref, bf16[128,32,128]{2,1,0:T(8,128)(2,1)S(1)} %all_to_all.16.recv_ref), custom_call_target="tpu_custom_call" | custom-call | tf_op jit(solution)/shard_map/place/pallas_call | solution.py:403
  95.8 12.5 %all-to-all-done.2 = f32[128,8,128]{2,1,0:T(8,128)S(1)} async-done(((f32[128,8,128]{2,1,0:T(8,128)}), f32[128,8,128]{2,1,0:T(8,128)S(1)}, u32[]{:S(2)}, u32[]{:S(2)}) %all-to-all-start.2) | async-done | bytes 524320 | tf_op jit(solution)/shard_map/all_to_all | solution.py:359
  108.3 0.1 slice.9
  108.4 0.7 copy.9
  109.0 0.7 slice.8
Async XLA Ops:
  2.0 0.9 copy-start
  2.9 1.0 copy-start.2
  3.9 1.0 copy-start.3
  5.0 0.7 copy-start.4
  7.4 33.5 %copy-start.1 = (bf16[4,128,128]{2,1,0:T(8,128)(2,1)S(1)}, bf16[4,128,128]{2,1,0:T(8,128)(2,1)}, u32[]{:S(2)}) copy-start(bf16[4,128,128]{2,1,0:T(8,128)(2,1)} %weights_ref.3) | copy-start | bytes 393220
  7.4 33.5 %copy-start.5 = (f32[8,128]{1,0:T(8,128)S(1)}, f32[8,128]{1,0:T(8,128)}, u32[]{:S(2)}) copy-start(f32[8,128]{1,0:T(8,128)} %vup_ref.3) | copy-start | bytes 12292
  90.6 17.7 %all-to-all-start.2 = ((f32[128,8,128]{2,1,0:T(8,128)}), f32[128,8,128]{2,1,0:T(8,128)S(1)}, u32[]{:S(2)}, u32[]{:S(2)}) async-start(f32[128,8,128]{2,1,0:T(8,128)} %sum_pieces.1), calls=%async_computation.2 | async-start | bytes 1048576 | tf_op jit(solution)/shard_map/all_to_all | solution.py:359
